TPU v7x, 32 devices: a whole 2x2x4 slice. The times are simulated.
32 devices in a mesh: dp: 4 (over y, core), mp: 8 (over z, x).
Axes of the slice: x: 2, y: 2, z: 4, core: 2. Of those that a mesh axis runs over, the one named last changes fastest.
Arguments:
- tokens: bfloat16 [4096, 2048], P(('dp', 'mp')), may hold values from -6 to 6
- norm_gain: float32 [2048], replicated, may hold values from 0.1 to 1.9
- router: bfloat16 [2048, 8], replicated, may hold values from -0.125 to 0.125
- routes: int32 [4096, 2], P(('dp', 'mp')), may hold values from 0 to 7, all different within a row; in each aligned block of 128 rows (0 to 127, 128 to 255, ...) at most 40 rows name the same one
- prompt_lengths: int32 [8], replicated, may hold values from 256 to 512, as said below
- wq_train: float32 [8, 2048, 2048], P(None, ('dp', 'mp'))
- wo_train: float32 [8, 2048, 2048], P(None, ('dp', 'mp')), may hold values from -0.25 to 0.25
- wkv_train: float32 [2048, 4096], P(('dp', 'mp'))
- page_table: int32 [4, 8, 8], P('dp', 'mp'), may hold values from 0 to 127, as said below
Outputs:
- attn_out: bfloat16 [4096, 2048], P(('dp', 'mp'))
- kv_pool: bfloat16 [512, 16, 4096], P(('dp', 'mp'))
Inputs may be any that keep to these rules, and one draw needn't show every extreme that they name: `routes`: each of the two entries of a row names a different expert; in the rows of one device (aligned blocks of 128 rows) no expert is named by more than 40 rows, a bound that some block reaches. `prompt_lengths`: every prompt uses at least 256 slots; some prompt uses all 512 and another exactly 256. `page_table`: entry [g, w, q] equals owner * 16 + w * 2 + c with c < 2; the pairs (owner, c) of one writer w in one group are distinct, so at most 2 pages of one writer go to one owner. In every group one owner receives 2 pages from every writer. Pool pages that no entry names stay zero.
All inputs are finite; a program needn't handle non-finite values.
Results may differ from a plain program's by a relative error of at most 0.012.
The roundings to bfloat16 on the way count: a program that leaves them out, or rounds other values in their place, can miss the bound.
Values may be sent and summed in bfloat16 or wider, within the bound.
A program may use at most 192 MiB of HBM per device.

v0:
```python
import jax
import jax.numpy as jnp
from jax import lax
from jax.sharding import PartitionSpec as P

HD = 128
PAGE = 16
PCAP = 2


def rotate(vectors, positions):
    half_dim = vectors.shape[-1] // 2
    frequency = 10000.0 ** (-(jnp.arange(half_dim, dtype=jnp.float32) * 2.0 / vectors.shape[-1]))
    angles = positions.astype(jnp.float32)[:, None] * frequency[None, :]
    cosine = jnp.cos(angles)[:, None, :]
    sine = jnp.sin(angles)[:, None, :]
    leading = vectors[..., :half_dim]
    trailing = vectors[..., half_dim:]
    return jnp.concatenate(
        [leading * cosine - trailing * sine, trailing * cosine + leading * sine], axis=-1
    )


def on_device(
    tokens, norm_gain, router, routes, prompt_lengths, wq_train, wo_train, wkv_train, page_table
):
    mp_count = lax.axis_size("mp")
    experts = wq_train.shape[0]
    blocks = mp_count // experts
    width = wq_train.shape[2]
    block_width = width // blocks
    head_dim = HD
    block_heads = block_width // head_dim
    tok_rows = tokens.shape[0]
    model_width = tokens.shape[1]
    capacity = tok_rows // 4 + tok_rows // 16
    prompt_len = tok_rows * mp_count // 2
    writer_pages = tok_rows * blocks // PAGE
    slot_count = mp_count * PCAP
    device = lax.axis_index("mp")
    expert = device // blocks
    prompt_group = lax.axis_index("dp")
    shard_rows = wq_train.shape[1]
    query_part = wq_train.reshape(experts, shard_rows, blocks, block_width).transpose(0, 2, 1, 3)
    query_part = query_part.reshape(mp_count, shard_rows, block_width).astype(jnp.bfloat16)
    output_part = wo_train.reshape(experts, shard_rows, blocks, block_width).transpose(0, 2, 1, 3)
    output_part = output_part.reshape(mp_count, shard_rows, block_width).astype(jnp.bfloat16)
    pair_part = wkv_train.reshape(shard_rows, 2, blocks, block_width).transpose(2, 0, 1, 3)
    pair_part = pair_part.reshape(blocks, shard_rows, 2 * block_width)
    pair_part = jnp.broadcast_to(pair_part[None], (experts, blocks, shard_rows, 2 * block_width))
    pair_part = pair_part.reshape(mp_count, shard_rows, 2 * block_width).astype(jnp.bfloat16)
    exchanged = (
        lax.all_to_all(query_part, "mp", split_axis=0, concat_axis=1, tiled=True),
        lax.all_to_all(output_part, "mp", split_axis=0, concat_axis=1, tiled=True),
        lax.all_to_all(pair_part, "mp", split_axis=0, concat_axis=1, tiled=True),
    )
    query_w, output_w, pair_w = (
        lax.all_gather(exchanged[0], "dp", axis=1, tiled=True),
        lax.all_gather(exchanged[1], "dp", axis=1, tiled=True),
        lax.all_gather(exchanged[2], "dp", axis=1, tiled=True),
    )
    query_w = query_w[0]
    output_w = output_w[0]
    pair_w = pair_w[0]
    wide_tokens = tokens.astype(jnp.float32)
    normed = (
        wide_tokens
        * lax.rsqrt(jnp.mean(wide_tokens * wide_tokens, axis=-1, keepdims=True) + 1e-06)
        * norm_gain
    ).astype(jnp.bfloat16)
    logits = jnp.dot(normed, router, preferred_element_type=jnp.float32)
    labels = jnp.arange(experts, dtype=jnp.int32)
    first_hot = routes[:, 0][None, :] == labels[:, None]
    second_hot = routes[:, 1][None, :] == labels[:, None]
    first_logit = jnp.sum(jnp.where(first_hot.T, logits, 0.0), axis=1)
    second_logit = jnp.sum(jnp.where(second_hot.T, logits, 0.0), axis=1)
    gate_first = 1.0 / (1.0 + jnp.exp(second_logit - first_logit))
    gate_second = 1.0 / (1.0 + jnp.exp(first_logit - second_logit))
    gates = jnp.where(
        first_hot, gate_first[None, :], jnp.where(second_hot, gate_second[None, :], 0.0)
    )
    named = first_hot | second_hot
    ranking = jnp.cumsum(named.astype(jnp.int32), axis=1) - 1
    chosen = named[:, None, :] & (
        ranking[:, None, :] == jnp.arange(capacity, dtype=jnp.int32)[None, :, None]
    )
    slot_row = jnp.sum(
        jnp.where(chosen, jnp.arange(tok_rows, dtype=jnp.int32)[None, None, :], 0), axis=-1
    )
    filled = jnp.any(chosen, axis=-1)
    picked = jnp.where(filled[..., None], normed[slot_row], jnp.zeros((), jnp.bfloat16))
    outgoing = jnp.broadcast_to(picked[:, None], (experts, blocks, capacity, model_width)).reshape(
        mp_count, capacity, model_width
    )
    places = jnp.where(filled, (device * tok_rows + slot_row) % prompt_len, 0)
    outgoing_places = jnp.broadcast_to(places[:, None], (experts, blocks, capacity)).reshape(
        mp_count, capacity
    )
    arrived = lax.all_to_all(outgoing, "mp", split_axis=0, concat_axis=0, tiled=True)
    arrived_places = lax.all_to_all(outgoing_places, "mp", split_axis=0, concat_axis=0, tiled=True)
    segment = lax.all_gather(normed, "mp", axis=0, tiled=True)
    projected = jnp.dot(segment, pair_w, preferred_element_type=jnp.float32)
    row_places = jnp.arange(segment.shape[0], dtype=jnp.int32) % prompt_len
    keyed = rotate(
        projected[:, :block_width].reshape(-1, block_heads, head_dim), row_places
    ).reshape(-1, block_width)
    kv_rows = jnp.concatenate([keyed, projected[:, block_width:]], axis=1).astype(jnp.bfloat16)
    own_pages = lax.dynamic_slice_in_dim(
        kv_rows, expert * writer_pages * PAGE, writer_pages * PAGE, 0
    )
    own_pages = own_pages.reshape(writer_pages, PAGE, 2 * block_width)
    page_ids = page_table[0, 0]
    target_cells = page_ids // slot_count * PCAP + page_ids % PCAP
    placing = (
        target_cells[None, :] == jnp.arange(mp_count * PCAP, dtype=jnp.int32)[:, None]
    ).astype(jnp.bfloat16)
    outgoing_pages = jnp.einsum(
        "cq,qpk->cpk", placing, own_pages, preferred_element_type=jnp.float32
    ).astype(jnp.bfloat16)
    outgoing_pages = outgoing_pages.reshape(mp_count, PCAP, PAGE, 2 * block_width)
    page_pool = lax.all_to_all(outgoing_pages, "mp", split_axis=0, concat_axis=0, tiled=True)
    queries = jnp.dot(arrived.reshape(-1, model_width), query_w, preferred_element_type=jnp.float32)
    query_places = arrived_places.reshape(-1)
    queries = (
        rotate(queries.reshape(-1, block_heads, head_dim), query_places) * head_dim ** (-0.5)
    ).astype(jnp.bfloat16)
    key_side = (
        kv_rows[:, :block_width].reshape(2, prompt_len, block_heads, head_dim).transpose(0, 2, 1, 3)
    )
    value_side = (
        kv_rows[:, block_width:].reshape(2, prompt_len, block_heads, head_dim).transpose(0, 2, 1, 3)
    )
    key_index = jnp.arange(prompt_len, dtype=jnp.int32)
    half_rows = mp_count // 2 * capacity
    sides = []
    for side in range(2):
        side_places = query_places[side * half_rows : (side + 1) * half_rows]
        length = prompt_lengths[2 * prompt_group + side]
        allowed = (key_index[None, :] <= side_places[:, None]) & (key_index[None, :] < length)
        side_queries = queries[side * half_rows : (side + 1) * half_rows].transpose(1, 0, 2)

        def one_head(operands):
            query_head, key_head, value_head = operands
            scores = lax.dot_general(
                query_head, key_head, (((1,), (1,)), ((), ())), preferred_element_type=jnp.float32
            )
            scores = jnp.where(allowed, scores, -jnp.inf)
            highest = jnp.max(scores, axis=-1, keepdims=True)
            powered = jnp.exp(scores - highest)
            softened = (powered / jnp.sum(powered, axis=-1, keepdims=True)).astype(jnp.bfloat16)
            return jnp.dot(softened, value_head, preferred_element_type=jnp.float32).astype(
                jnp.bfloat16
            )

        sides.append(lax.map(one_head, (side_queries, key_side[side], value_side[side])))
    heads_out = jnp.stack(sides).transpose(0, 2, 1, 3).reshape(2 * half_rows, block_width)
    partial_value = lax.dot_general(
        heads_out, output_w, (((1,), (1,)), ((), ())), preferred_element_type=jnp.float32
    )
    partial_value = partial_value.astype(jnp.bfloat16).reshape(mp_count, capacity, model_width)
    returned = lax.all_to_all(partial_value, "mp", split_axis=0, concat_axis=0, tiled=True)
    page_pool = page_pool.reshape(slot_count, PAGE, 2 * block_width)
    summed = (
        returned.astype(jnp.float32).reshape(experts, blocks, capacity, model_width).sum(axis=1)
    )
    summed = summed.reshape(experts * capacity, model_width)
    weights = jnp.where(chosen, gates[:, None, :], 0.0).reshape(experts * capacity, tok_rows)
    mixed = lax.dot_general(
        weights,
        summed,
        (((0,), (0,)), ((), ())),
        precision=lax.Precision.HIGHEST,
        preferred_element_type=jnp.float32,
    )
    return (mixed.astype(jnp.bfloat16), page_pool)


def solution(mesh):
    placed = (
        P(("dp", "mp"), None),
        P(),
        P(),
        P(("dp", "mp"), None),
        P(),
        P(None, ("dp", "mp"), None),
        P(None, ("dp", "mp"), None),
        P(("dp", "mp"), None),
        P("dp", "mp", None),
    )
    return jax.shard_map(
        on_device,
        mesh=mesh,
        in_specs=placed,
        out_specs=(P(("dp", "mp"), None), P(("dp", "mp"), None, None)),
        check_vma=False,
    )
```

profile of v0, /device:TPU:0, one launch (start us, length us, event | category | flops | bytes accessed | tf_op | source)
XLA Modules:
  0.0 570.2 jit_solution(986742737802211337)
XLA Ops:
  7.2 2.5 convert_element_type.76
  9.7 55.3 %all_to_all.57 = bf16[8,64,2048]{2,1,0:T(8,128)(2,1)S(1)} all-to-all(bf16[8,64,2048]{2,1,0:T(8,128)(2,1)S(1)} %convert_element_type.76), channel_id=1, replica_groups=mesh['dp'=4,'mp'=8] {'mp'}, dimensions={0} | all-to-all | bytes 4194304 | tf_op jit(solution)/shard_map/all_to_all | solution.py:53
  71.3 4.8 all-to-all-start.3
  77.4 127.0 %all-to-all-done.3 = bf16[8,64,4096]{2,1,0:T(8,128)(2,1)} async-done(((bf16[8,64,4096]{2,1,0:T(8,128)(2,1)}), bf16[8,64,4096]{2,1,0:T(8,128)(2,1)}, u32[]{:S(2)}, u32[]{:S(2)}) %all-to-all-start.3) | async-done | bytes 4194336 | tf_op jit(solution)/shard_map/all_to_all | solution.py:55
  205.8 3.3 all-to-all-start.2
  209.1 3.8 convert_element_type.82
  212.9 2.7 all-to-all-done.2
  215.6 3.6 all-to-all-start.4
  219.3 3.0 gather_fusion
  222.3 2.5 broadcast_select_fusion
  224.9 41.1 %all-to-all-done.4 = bf16[8,64,2048]{2,1,0:T(8,128)(2,1)S(1)} async-done(((bf16[8,64,2048]{2,1,0:T(8,128)(2,1)}), bf16[8,64,2048]{2,1,0:T(8,128)(2,1)S(1)}, u32[]{:S(2)}, u32[]{:S(2)}) %all-to-all-start.4) | async-done | bytes 2097184 | tf_op jit(solution)/shard_map/all_to_all | solution.py:54
  266.0 4.3 all-to-all-start
  272.7 3.0 multiply_cosine_fusion
  276.6 24.6 %all-to-all-done = bf16[8,40,2048]{2,1,0:T(8,128)(2,1)} async-done(((bf16[8,40,2048]{2,1,0:T(8,128)(2,1)}), bf16[8,40,2048]{2,1,0:T(8,128)(2,1)}, u32[]{:S(2)}, u32[]{:S(2)}) %all-to-all-start) | async-done | bytes 1310752 | tf_op jit(solution)/shard_map/all_to_all | solution.py:99
  301.3 5.9 %fusion.72 = f32[320,16,128]{2,0,1:T(8,128)S(1)} fusion(bf16[320,2048,1]{1,0,2:T(8,128)(2,1)} %bitcast.5, bf16[16,128,2048]{2,1,0:T(8,128)(2,1)} %bitcast.168), kind=kOutput, calls=%fused_computation.142 | convolution fusion | flops 2684354560 | bytes 12320768 | tf_op jit(solution)/shard_map/dot_general | solution.py:122
  310.3 15.8 %all-gather.9.cloned.1.call-done = bf16[1,2048,4096]{2,1,0:T(8,128)(2,1)} async-done(((bf16[1,512,4096]{2,1,0:T(8,128)(2,1)}), bf16[1,2048,4096]{2,1,0:T(8,128)(2,1)}) %all-gather.9.cloned.1.call-update) | async-done | bytes 16777232 | tf_op jit(solution)/shard_map/all_gather | solution.py:60
  326.2 23.4 %fusion.32 = f32[1024,4096]{1,0:T(8,128)} fusion(bf16[1024,2048]{1,0:T(8,128)(2,1)} %all-gather.7.cloned.1.call-done, bf16[1,2048,4096]{2,1,0:T(8,128)(2,1)} %all-gather.9.cloned.1.call-done), kind=kOutput, calls=%fused_computation.41 | convolution fusion | flops 17179869184 | bytes 37748736 | tf_op jit(solution)/shard_map/dot_general | solution.py:102
  349.6 4.1 slice_bitcast_fusion
  353.6 4.4 slice_bitcast_fusion.9
  360.0 4.3 subtract_convert_fusion
  375.5 42.7 %while.22 = (s32[]{:T(128)}, bf16[16,160,128]{2,1,0:T(8,128)(2,1)S(1)}, bf16[16,160,128]{2,1,0:T(8,128)(2,1)}, bf16[16,512,128]{2,1,0:T(8,128)(2,1)}, bf16[16,51...) while((s32[]{:T(128)}, ...), condition=%wide.region_9.10_spmd.clone, body=%wide.region_6.9_spmd.clone.sunk | while | flops 42700480 | bytes 1334357 | solution.py:155
  420.2 42.7 %while.23 = (s32[]{:T(128)}, bf16[16,160,128]{2,1,0:T(8,128)(2,1)S(1)}, bf16[16,160,128]{2,1,0:T(8,128)(2,1)}, bf16[16,512,128]{2,1,0:T(8,128)(2,1)}, bf16[16,51...) while((s32[]{:T(128)}, ...), condition=%wide.region_13.14_spmd.clone, body=%wide.region_10.13_spmd.clone.sunk | while | flops 42700480 | bytes 1334357 | solution.py:155
  463.5 7.4 %fusion.36 = bf16[320,2048]{1,0:T(8,128)(2,1)} fusion(bf16[1,2048,2048]{2,1,0:T(8,128)(2,1)} %all-gather.11.cloned.1.call-done, bf16[40,8,16,128]{3,2,1,0:T(8,128)(2,1)S(1)} %bitcast.167), kind=kOutput, calls=%fused_computation.55 | convolution fusion | flops 2685009920 | bytes 11010048 | tf_op jit(solution)/shard_map/dot_general | solution.py:157
  470.9 5.9 %all-to-all-start.5 = ((bf16[8,40,2048]{2,1,0:T(8,128)(2,1)}), bf16[8,40,2048]{2,1,0:T(8,128)(2,1)}, u32[]{:S(2)}, u32[]{:S(2)}) async-start(bf16[8,40,2048]{2,1,0:T(8,128)(2,1)} %bitcast.32), calls=%async_computation.5 | async-start | bytes 2621440 | tf_op jit(solution)/shard_map/all_to_all | solution.py:161
  476.9 4.2 slice.107
  485.1 2.6 reshape.489
  487.7 5.6 copy.35
  493.3 15.4 %all-to-all-done.5 = bf16[8,40,2048]{2,1,0:T(8,128)(2,1)} async-done(((bf16[8,40,2048]{2,1,0:T(8,128)(2,1)}), bf16[8,40,2048]{2,1,0:T(8,128)(2,1)}, u32[]{:S(2)}, u32[]{:S(2)}) %all-to-all-start.5) | async-done | bytes 1310752 | tf_op jit(solution)/shard_map/all_to_all | solution.py:161
  508.7 3.6 all-to-all-start.6
  512.6 3.2 fusion.40
  515.8 45.0 %all-to-all-done.6 = bf16[8,2,16,4096]{3,1,2,0:T(2,128)(2,1)S(1)} async-done(((bf16[8,2,16,4096]{3,1,2,0:T(2,128)(2,1)}), bf16[8,2,16,4096]{3,1,2,0:T(2,128)(2,1)S(1)}, u32[]{:S(2)}, u32[]{:S(2)}) %all-to-all-start.6) | async-done | bytes 2097184 | tf_op jit(solution)/shard_map/all_to_all | solution.py:121
  560.8 2.6 copy.36
  (178 shorter events, 120.1 us)
Async XLA Ops:
  7.2 505.2 %copy-start = (bf16[2048,8]{0,1:T(8,128)(2,1)S(1)}, bf16[2048,8]{0,1:T(8,128)(2,1)}, u32[]{:S(2)}) copy-start(bf16[2048,8]{0,1:T(8,128)(2,1)} %param.15) | copy-start | bytes 98308
  7.2 294.1 %all-gather.5.cloned.1.call-start = ((), (), s32[]{:S(2)}) async-start(), calls=%async_computation.7 | async-start | bytes 10485760 | tf_op jit(solution)/shard_map/all_gather | solution.py:58
  67.5 1.2 copy-start.6
  71.3 4.8 copy-start.5
  71.3 5.1 copy-start.7
  71.3 133.1 %all-to-all-start.3 = ((bf16[8,64,4096]{2,1,0:T(8,128)(2,1)}), bf16[8,64,4096]{2,1,0:T(8,128)(2,1)}, u32[]{:S(2)}, u32[]{:S(2)}) async-start(bf16[8,64,4096]{2,1,0:T(8,128)(2,1)} %reshape.481), calls=%async_computation.3 | async-start | bytes 8388608 | tf_op jit(solution)/shard_map/all_to_all | solution.py:55
  76.1 234.3 %all-gather.7.cloned.1.call-start = ((), (), s32[]{:S(2)}) async-start(), calls=%async_computation.8 | async-start | bytes 4718592 | tf_op jit(solution)/shard_map/all_gather | solution.py:101
  77.3 127.1 %copy-start.9 = (s32[128,2]{0,1:T(2,128)S(1)}, s32[128,2]{0,1:T(2,128)}, u32[]{:S(2)}) copy-start(s32[128,2]{0,1:T(2,128)} %param.16) | copy-start | bytes 3076
  77.3 248.8 %all-gather.9.cloned.1.call-start = ((), (), s32[]{:S(2)}) async-start(), calls=%async_computation.9 | async-start | bytes 20971520 | tf_op jit(solution)/shard_map/all_gather | solution.py:60
  205.8 9.8 %all-to-all-start.2 = ((s32[8,1,40]{2,1,0:T(1,128)}), s32[8,1,40]{2,1,0:T(1,128)S(1)}, u32[]{:S(2)}, u32[]{:S(2)}) async-start(s32[8,1,40]{2,1,0:T(1,128)} %bitcast.12), calls=%async_computation.2 | async-start | bytes 8192 | tf_op jit(solution)/shard_map/all_to_all | solution.py:100
  212.9 6.4 %copy-start.1 = (bf16[128,2048]{1,0:T(8,128)(2,1)S(1)}, bf16[128,2048]{1,0:T(8,128)(2,1)}, u32[]{:S(2)}) copy-start(bf16[128,2048]{1,0:T(8,128)(2,1)} %fusion.46) | copy-start | bytes 1572868
  215.6 50.4 %all-to-all-start.4 = ((bf16[8,64,2048]{2,1,0:T(8,128)(2,1)}), bf16[8,64,2048]{2,1,0:T(8,128)(2,1)S(1)}, u32[]{:S(2)}, u32[]{:S(2)}) async-start(bf16[8,64,2048]{2,1,0:T(8,128)(2,1)} %convert_element_type.82), calls=%async_computation.4 | async-start | bytes 4194304 | tf_op jit(solution)/shard_map/all_to_all | solution.py:54
  222.3 48.4 %copy-start.8 = (s32[8]{0:T(128)S(1)}, s32[8]{0:T(128)}, u32[]{:S(2)}) copy-start(s32[8]{0:T(128)} %param.17) | copy-start | bytes 100
  266.0 10.7 %copy-start.4 = (bf16[8,64,2048]{2,1,0:T(8,128)(2,1)}, bf16[8,64,2048]{2,1,0:T(8,128)(2,1)S(1)}, u32[]{:S(2)}) copy-start(bf16[8,64,2048]{2,1,0:T(8,128)(2,1)S(1)} %all-to-all-done.4) | copy-start | bytes 6291460
  266.0 35.3 %all-to-all-start = ((bf16[8,40,2048]{2,1,0:T(8,128)(2,1)}), bf16[8,40,2048]{2,1,0:T(8,128)(2,1)}, u32[]{:S(2)}, u32[]{:S(2)}) async-start(bf16[8,40,2048]{2,1,0:T(8,128)(2,1)} %broadcast_select_fusion), calls=%async_computation | async-start | bytes 2621440 | tf_op jit(solution)/shard_map/all_to_all | solution.py:99
  270.2 193.3 %all-gather.11.cloned.1.call-start = ((), (), s32[]{:S(2)}) async-start(), calls=%async_computation.10 | async-start | bytes 10485760 | tf_op jit(solution)/shard_map/all_gather | solution.py:59
  366.7 1.9 copy-start.2
  470.9 5.9 %copy-start.10 = (s32[1,1,8]{2,1,0:T(1,128)S(1)}, s32[1,1,8]{2,1,0:T(1,128)}, u32[]{:S(2)}) copy-start(s32[1,1,8]{2,1,0:T(1,128)} %param.21) | copy-start | bytes 100
  470.9 37.8 %all-to-all-start.5 = ((bf16[8,40,2048]{2,1,0:T(8,128)(2,1)}), bf16[8,40,2048]{2,1,0:T(8,128)(2,1)}, u32[]{:S(2)}, u32[]{:S(2)}) async-start(bf16[8,40,2048]{2,1,0:T(8,128)(2,1)} %bitcast.32), calls=%async_computation.5 | async-start | bytes 2621440 | tf_op jit(solution)/shard_map/all_to_all | solution.py:161
  476.9 4.6 copy-start.3
  508.7 52.1 %all-to-all-start.6 = ((bf16[8,2,16,4096]{3,1,2,0:T(2,128)(2,1)}), bf16[8,2,16,4096]{3,1,2,0:T(2,128)(2,1)S(1)}, u32[]{:S(2)}, u32[]{:S(2)}) async-start(bf16[8,2,16,4096]{3,1,2,0:T(2,128)(2,1)} %copy.35), calls=%async_computation.6 | async-start | bytes 4194304 | tf_op jit(solution)/shard_map/all_to_all | solution.py:121
Sparse Core Ops, SparseCore 0:
  67.7 57.3 all-gather.4
  127.7 91.9 all-gather.6
  221.3 104.7 all-gather.8
  328.1 58.2 all-gather.10
where the time goes:
time: 576 us; the launch traced here: 570 us
  waiting for transfers between devices  272 us (47%)
  matrix products  119 us (21%)
  blocking collectives  55.3 us (10%)
  local copies, waits for them, and re-layouts  50.5 us (9%)
  other arithmetic  32.3 us (6%)
  starting transfers between devices  26.1 us (5%)
  between operations  14.4 us (2%)
    all_to_all x1, waiting for transfers between devices, on_device(): lax.all_to_all(pair_part, 'mp', split_axis=0, concat_axis=1, tiled=True)  127 us
    all_to_all x1, blocking collectives, on_device(): lax.all_to_all(query_part, 'mp', split_axis=0, concat_axis=1, tiled=True)  55.3 us
    all_to_all x1, waiting for transfers between devices, on_device(): lax.all_to_all(outgoing_pages, 'mp', split_axis=0, concat_axis=0, tiled=T...  45 us
    all_to_all x1, waiting for transfers between devices, on_device(): lax.all_to_all(output_part, 'mp', split_axis=0, concat_axis=1, tiled=True)  41.1 us
    dot_general x32, matrix products, one_head(): lax.dot_general(query_head, key_head, (((1,), (1,)), ((), ())), preferred...  39.8 us
    dot_general x32, matrix products, one_head(): jnp.dot(softened, value_head, preferred_element_type=jnp.float32)  37.8 us
    all_to_all x1, waiting for transfers between devices, on_device(): lax.all_to_all(outgoing, 'mp', split_axis=0, concat_axis=0, tiled=True)  24.6 us
    dot_general x1, matrix products, on_device(): projected = jnp.dot(segment, pair_w, preferred_element_type=jnp.float32)  23.4 us
  transfers between devices with their start and end apart: 10, of which 7 were waited for; matrix products, arithmetic and copies ran while one was open for 32% of the time, Pallas kernels for 0%

commit v1 on v0

--- a/solution.py
+++ b/solution.py
@@ -6,6 +6,22 @@
 HD = 128
 PAGE = 16
 PCAP = 2
+
+
+def pairwise_exchange(x, axis, split, join):
+    ways, here = (lax.axis_size(axis), lax.axis_index(axis))
+    width = x.shape[split] // ways
+    dims = list(x.shape)
+    dims[split] = width
+    height = dims[join]
+    dims[join] = height * ways
+    full = jnp.zeros(dims, x.dtype)
+    for mask in range(ways):
+        part = lax.dynamic_slice_in_dim(x, (here ^ mask) * width, width, axis=split)
+        if mask:
+            part = lax.ppermute(part, axis, [(d, d ^ mask) for d in range(ways)])
+        full = lax.dynamic_update_slice_in_dim(full, part, (here ^ mask) * height, axis=join)
+    return full
 
 
 def rotate(vectors, positions):
@@ -118,7 +134,7 @@
         "cq,qpk->cpk", placing, own_pages, preferred_element_type=jnp.float32
     ).astype(jnp.bfloat16)
     outgoing_pages = outgoing_pages.reshape(mp_count, PCAP, PAGE, 2 * block_width)
-    page_pool = lax.all_to_all(outgoing_pages, "mp", split_axis=0, concat_axis=0, tiled=True)
+    page_pool = pairwise_exchange(outgoing_pages, "mp", 0, 0)
     queries = jnp.dot(arrived.reshape(-1, model_width), query_w, preferred_element_type=jnp.float32)
     query_places = arrived_places.reshape(-1)
     queries = (

time: 576 us -> 567 us (0.984)
  the two profiles are of different devices: /device:TPU:0 before, /device:TPU:8 now
where the time goes in v1:
time: 567 us; the launch traced here: 559 us
  waiting for transfers between devices  246 us (43%)
  matrix products  119 us (21%)
  local copies, waits for them, and re-layouts  53.9 us (10%)
  blocking collectives  53.4 us (9%)
  starting transfers between devices  41.3 us (7%)
  other arithmetic  30.5 us (5%)
  between operations  14.5 us (3%)
    all_to_all x1, waiting for transfers between devices, on_device(): lax.all_to_all(pair_part, 'mp', split_axis=0, concat_axis=1, tiled=True)  123 us
    all_to_all x1, blocking collectives, on_device(): lax.all_to_all(query_part, 'mp', split_axis=0, concat_axis=1, tiled=True)  53.4 us
    ppermute x7, waiting for transfers between devices, pairwise_exchange(): part = lax.ppermute(part, axis, [(d, d ^ mask) for d in range(ways)])  42.1 us
    dot_general x32, matrix products, one_head(): lax.dot_general(query_head, key_head, (((1,), (1,)), ((), ())), preferred...  39.8 us
    dot_general x32, matrix products, one_head(): jnp.dot(softened, value_head, preferred_element_type=jnp.float32)  37.8 us
    all_to_all x1, waiting for transfers between devices, on_device(): lax.all_to_all(output_part, 'mp', split_axis=0, concat_axis=1, tiled=True)  37.4 us
    dot_general x1, matrix products, on_device(): projected = jnp.dot(segment, pair_w, preferred_element_type=jnp.float32)  23.6 us
    all_to_all x1, waiting for transfers between devices, on_device(): lax.all_to_all(outgoing, 'mp', split_axis=0, concat_axis=0, tiled=True)  22.9 us
  transfers between devices with their start and end apart: 16, of which 7 were waited for; matrix products, arithmetic and copies ran while one was open for 35% of the time, Pallas kernels for 0%

profile of v1, /device:TPU:8, one launch (start us, length us, event | category | flops | bytes accessed | tf_op | source)
XLA Modules:
  0.0 559.3 jit_solution(15432991972636414642)
XLA Ops:
  7.2 2.5 convert_element_type.76
  9.7 53.4 %all_to_all.52 = bf16[8,64,2048]{2,1,0:T(8,128)(2,1)S(1)} all-to-all(bf16[8,64,2048]{2,1,0:T(8,128)(2,1)S(1)} %convert_element_type.76), channel_id=1, replica_groups=mesh['dp'=4,'mp'=8] {'mp'}, dimensions={0} | all-to-all | bytes 4194304 | tf_op jit(solution)/shard_map/all_to_all | solution.py:69
  63.1 2.5 copy.49
  65.7 2.5 reshape.481
  68.2 5.6 %all-to-all-start.3 = ((bf16[8,64,4096]{2,1,0:T(8,128)(2,1)}), bf16[8,64,4096]{2,1,0:T(8,128)(2,1)}, u32[]{:S(2)}, u32[]{:S(2)}) async-start(bf16[8,64,4096]{2,1,0:T(8,128)(2,1)} %reshape.481), calls=%async_computation.3 | async-start | bytes 8388608 | tf_op jit(solution)/shard_map/all_to_all | solution.py:71
  75.1 123.4 %all-to-all-done.3 = bf16[8,64,4096]{2,1,0:T(8,128)(2,1)} async-done(((bf16[8,64,4096]{2,1,0:T(8,128)(2,1)}), bf16[8,64,4096]{2,1,0:T(8,128)(2,1)}, u32[]{:S(2)}, u32[]{:S(2)}) %all-to-all-start.3) | async-done | bytes 4194336 | tf_op jit(solution)/shard_map/all_to_all | solution.py:71
  199.9 7.0 %all-to-all-start.2 = ((s32[8,1,40]{2,1,0:T(1,128)}), s32[8,1,40]{2,1,0:T(1,128)S(1)}, u32[]{:S(2)}, u32[]{:S(2)}) async-start(s32[8,1,40]{2,1,0:T(1,128)} %bitcast.12), calls=%async_computation.2 | async-start | bytes 8192 | tf_op jit(solution)/shard_map/all_to_all | solution.py:116
  206.8 3.8 convert_element_type.82
  212.0 5.0 all-to-all-start.4
  217.1 3.0 gather_fusion
  220.1 2.5 broadcast_select_fusion
  222.6 37.4 %all-to-all-done.4 = bf16[8,64,2048]{2,1,0:T(8,128)(2,1)S(1)} async-done(((bf16[8,64,2048]{2,1,0:T(8,128)(2,1)}), bf16[8,64,2048]{2,1,0:T(8,128)(2,1)S(1)}, u32[]{:S(2)}, u32[]{:S(2)}) %all-to-all-start.4) | async-done | bytes 2097184 | tf_op jit(solution)/shard_map/all_to_all | solution.py:70
  260.0 7.9 %all-to-all-start = ((bf16[8,40,2048]{2,1,0:T(8,128)(2,1)}), bf16[8,40,2048]{2,1,0:T(8,128)(2,1)}, u32[]{:S(2)}, u32[]{:S(2)}) async-start(bf16[8,40,2048]{2,1,0:T(8,128)(2,1)} %broadcast_select_fusion), calls=%async_computation | async-start | bytes 2621440 | tf_op jit(solution)/shard_map/all_to_all | solution.py:115
  272.9 22.9 %all-to-all-done = bf16[8,40,2048]{2,1,0:T(8,128)(2,1)} async-done(((bf16[8,40,2048]{2,1,0:T(8,128)(2,1)}), bf16[8,40,2048]{2,1,0:T(8,128)(2,1)}, u32[]{:S(2)}, u32[]{:S(2)}) %all-to-all-start) | async-done | bytes 1310752 | tf_op jit(solution)/shard_map/all_to_all | solution.py:115
  295.8 6.0 %fusion.72 = f32[320,16,128]{2,0,1:T(8,128)S(1)} fusion(bf16[320,2048,1]{1,0,2:T(8,128)(2,1)} %bitcast.5, bf16[16,128,2048]{2,1,0:T(8,128)(2,1)} %bitcast.168), kind=kOutput, calls=%fused_computation.158 | convolution fusion | flops 2684354560 | bytes 12320768 | tf_op jit(solution)/shard_map/dot_general | solution.py:138
  305.0 18.4 %all-gather.9.cloned.1.call-done = bf16[1,2048,4096]{2,1,0:T(8,128)(2,1)} async-done(((bf16[1,512,4096]{2,1,0:T(8,128)(2,1)}), bf16[1,2048,4096]{2,1,0:T(8,128)(2,1)}) %all-gather.9.cloned.1.call-update) | async-done | bytes 16777232 | tf_op jit(solution)/shard_map/all_gather | solution.py:76
  323.4 23.6 %fusion.32 = f32[1024,4096]{1,0:T(8,128)} fusion(bf16[1024,2048]{1,0:T(8,128)(2,1)} %all-gather.7.cloned.1.call-done, bf16[1,2048,4096]{2,1,0:T(8,128)(2,1)} %all-gather.9.cloned.1.call-done), kind=kOutput, calls=%fused_computation.41 | convolution fusion | flops 17179869184 | bytes 37748736 | tf_op jit(solution)/shard_map/dot_general | solution.py:118
  347.0 4.1 slice_bitcast_fusion
  351.1 4.0 slice.107
  355.1 6.3 %slice_bitcast_fusion.9 = bf16[128,8,16,128]{3,1,2,0:T(8,128)(2,1)} fusion(f32[1024,4096]{1,0:T(8,128)} %fusion.32), kind=kLoop, calls=%fused_computation.157 | loop fusion | bytes 8388608
  363.4 3.7 subtract_convert_fusion
  367.2 2.4 pad_maximum_fusion
  372.3 2.8 convolution_convert_fusion.2
  375.1 3.3 reshape.489
  378.4 3.2 constant_dynamic-slice_fusion
  385.2 2.4 collective-permute-start.3
  397.5 42.7 %while.22 = (s32[]{:T(128)}, bf16[16,160,128]{2,1,0:T(8,128)(2,1)S(1)}, bf16[16,160,128]{2,1,0:T(8,128)(2,1)}, bf16[16,512,128]{2,1,0:T(8,128)(2,1)}, bf16[16,51...) while((s32[]{:T(128)}, ...), condition=%wide.region_9.10_spmd.clone, body=%wide.region_6.9_spmd.clone.sunk | while | flops 42700480 | bytes 1334357 | solution.py:171
  442.1 42.7 %while.23 = (s32[]{:T(128)}, bf16[16,160,128]{2,1,0:T(8,128)(2,1)S(1)}, bf16[16,160,128]{2,1,0:T(8,128)(2,1)}, bf16[16,512,128]{2,1,0:T(8,128)(2,1)}, bf16[16,51...) while((s32[]{:T(128)}, ...), condition=%wide.region_13.14_spmd.clone, body=%wide.region_10.13_spmd.clone.sunk | while | flops 42700480 | bytes 1334357 | solution.py:171
  485.5 7.4 %fusion.36 = bf16[320,2048]{1,0:T(8,128)(2,1)} fusion(bf16[1,2048,2048]{2,1,0:T(8,128)(2,1)} %all-gather.11.cloned.1.call-done, bf16[40,8,16,128]{3,2,1,0:T(8,128)(2,1)S(1)} %bitcast.167), kind=kOutput, calls=%fused_computation.55 | convolution fusion | flops 2685009920 | bytes 11010048 | tf_op jit(solution)/shard_map/dot_general | solution.py:173
  492.9 5.4 all-to-all-start.5
  508.3 38.1 %collective-permute-done.5 = bf16[1,2,16,4096]{3,1,0,2:T(2,128)(2,1)S(1)} collective-permute-done((bf16[1,2,16,4096]{3,1,0,2:T(2,128)(2,1)S(1)}, bf16[1,2,16,4096]{3,1,0,2:T(2,128)(2,1)S(1)}, u32[]{:S(2)}, u32[]{:S(2)}) %collective-permute-start.5) | collective-permute-done | bytes 262176 | tf_op jit(solution)/shard_map/ppermute | solution.py:22
  546.6 3.9 collective-permute-done.6
  (208 shorter events, 129.6 us)
Async XLA Ops:
  7.2 262.6 %copy-start = (bf16[2048,8]{0,1:T(8,128)(2,1)S(1)}, bf16[2048,8]{0,1:T(8,128)(2,1)}, u32[]{:S(2)}) copy-start(bf16[2048,8]{0,1:T(8,128)(2,1)} %param.15) | copy-start | bytes 98308
  7.2 288.6 %all-gather.5.cloned.1.call-start = ((), (), s32[]{:S(2)}) async-start(), calls=%async_computation.6 | async-start | bytes 10485760 | tf_op jit(solution)/shard_map/all_gather | solution.py:74
  63.1 2.5 copy-start.9
  68.2 5.6 %copy-start.8 = (bf16[128,2048]{1,0:T(8,128)(2,1)S(1)}, bf16[128,2048]{1,0:T(8,128)(2,1)}, u32[]{:S(2)}) copy-start(bf16[128,2048]{1,0:T(8,128)(2,1)} %param.13) | copy-start | bytes 1572868
  68.2 5.8 %copy-start.12 = (f32[2048]{0:T(1024)S(1)}, f32[2048]{0:T(1024)}, u32[]{:S(2)}) copy-start(f32[2048]{0:T(1024)} %param.14) | copy-start | bytes 24580
  68.2 130.3 %all-to-all-start.3 = ((bf16[8,64,4096]{2,1,0:T(8,128)(2,1)}), bf16[8,64,4096]{2,1,0:T(8,128)(2,1)}, u32[]{:S(2)}, u32[]{:S(2)}) async-start(bf16[8,64,4096]{2,1,0:T(8,128)(2,1)} %reshape.481), calls=%async_computation.3 | async-start | bytes 8388608 | tf_op jit(solution)/shard_map/all_to_all | solution.py:71
  73.8 231.2 %all-gather.7.cloned.1.call-start = ((), (), s32[]{:S(2)}) async-start(), calls=%async_computation.7 | async-start | bytes 4718592 | tf_op jit(solution)/shard_map/all_gather | solution.py:117
  75.0 123.5 %copy-start.14 = (s32[128,2]{0,1:T(2,128)S(1)}, s32[128,2]{0,1:T(2,128)}, u32[]{:S(2)}) copy-start(s32[128,2]{0,1:T(2,128)} %param.16) | copy-start | bytes 3076
  75.0 248.4 %all-gather.9.cloned.1.call-start = ((), (), s32[]{:S(2)}) async-start(), calls=%async_computation.8 | async-start | bytes 20971520 | tf_op jit(solution)/shard_map/all_gather | solution.py:76
  199.9 12.1 %all-to-all-start.2 = ((s32[8,1,40]{2,1,0:T(1,128)}), s32[8,1,40]{2,1,0:T(1,128)S(1)}, u32[]{:S(2)}, u32[]{:S(2)}) async-start(s32[8,1,40]{2,1,0:T(1,128)} %bitcast.12), calls=%async_computation.2 | async-start | bytes 8192 | tf_op jit(solution)/shard_map/all_to_all | solution.py:116
  210.7 6.4 %copy-start.2 = (bf16[128,2048]{1,0:T(8,128)(2,1)S(1)}, bf16[128,2048]{1,0:T(8,128)(2,1)}, u32[]{:S(2)}) copy-start(bf16[128,2048]{1,0:T(8,128)(2,1)} %fusion.46) | copy-start | bytes 1572868
  212.0 48.1 %all-to-all-start.4 = ((bf16[8,64,2048]{2,1,0:T(8,128)(2,1)}), bf16[8,64,2048]{2,1,0:T(8,128)(2,1)S(1)}, u32[]{:S(2)}, u32[]{:S(2)}) async-start(bf16[8,64,2048]{2,1,0:T(8,128)(2,1)} %convert_element_type.82), calls=%async_computation.4 | async-start | bytes 4194304 | tf_op jit(solution)/shard_map/all_to_all | solution.py:70
  220.1 47.8 %copy-start.13 = (s32[8]{0:T(128)S(1)}, s32[8]{0:T(128)}, u32[]{:S(2)}) copy-start(s32[8]{0:T(128)} %param.17) | copy-start | bytes 100
  220.1 49.9 %copy-start.15 = (s32[1,1,8]{2,1,0:T(1,128)S(1)}, s32[1,1,8]{2,1,0:T(1,128)}, u32[]{:S(2)}) copy-start(s32[1,1,8]{2,1,0:T(1,128)} %param.21) | copy-start | bytes 100
  260.0 12.9 %copy-start.6 = (bf16[8,64,2048]{2,1,0:T(8,128)(2,1)}, bf16[8,64,2048]{2,1,0:T(8,128)(2,1)S(1)}, u32[]{:S(2)}) copy-start(bf16[8,64,2048]{2,1,0:T(8,128)(2,1)S(1)} %all-to-all-done.4) | copy-start | bytes 6291460
  260.0 35.8 %all-to-all-start = ((bf16[8,40,2048]{2,1,0:T(8,128)(2,1)}), bf16[8,40,2048]{2,1,0:T(8,128)(2,1)}, u32[]{:S(2)}, u32[]{:S(2)}) async-start(bf16[8,40,2048]{2,1,0:T(8,128)(2,1)} %broadcast_select_fusion), calls=%async_computation | async-start | bytes 2621440 | tf_op jit(solution)/shard_map/all_to_all | solution.py:115
  267.9 217.7 %all-gather.11.cloned.1.call-start = ((), (), s32[]{:S(2)}) async-start(), calls=%async_computation.9 | async-start | bytes 10485760 | tf_op jit(solution)/shard_map/all_gather | solution.py:75
  369.5 2.7 copy-start.3
  378.4 10.5 %copy-start.4 = (bf16[1024,16,128]{2,1,0:T(8,128)(2,1)S(1)}, bf16[1024,16,128]{2,1,0:T(8,128)(2,1)}, u32[]{:S(2)}) copy-start(bf16[1024,16,128]{2,1,0:T(8,128)(2,1)} %copy-done.3) | copy-start | bytes 12582916
  381.7 118.0 %collective-permute-start = (bf16[1,2,16,4096]{3,1,0,2:T(2,128)(2,1)}, bf16[1,2,16,4096]{3,1,0,2:T(2,128)(2,1)}, u32[]{:S(2)}, u32[]{:S(2)}) collective-permute-start(bf16[1,2,16,4096]{3,1,0,2:T(2,128)(2,1)} %get-tuple-element.196), channel_id=1, source_target_pairs={{0,1},{1,0},{2,3},{3,2},{4,5},{5,4},{6,7},{7,6},{8,9},{9,8},{10,11... | collective-permute-start | bytes 786440 | tf_op jit(solution)/shard_map/ppermute | solution.py:22
  383.1 119.2 %collective-permute-start.1 = (bf16[1,2,16,4096]{3,1,0,2:T(2,128)(2,1)}, bf16[1,2,16,4096]{3,1,0,2:T(2,128)(2,1)}, u32[]{:S(2)}, u32[]{:S(2)}) collective-permute-start(bf16[1,2,16,4096]{3,1,0,2:T(2,128)(2,1)} %get-tuple-element.195), channel_id=1, source_target_pairs={{0,2},{1,3},{2,0},{3,1},{4,6},{5,7},{6,4},{7,5},{8,10},{9,11},{10,... | collective-permute-start | bytes 786440 | tf_op jit(solution)/shard_map/ppermute | solution.py:22
  383.6 121.3 %collective-permute-start.2 = (bf16[1,2,16,4096]{3,1,0,2:T(2,128)(2,1)}, bf16[1,2,16,4096]{3,1,0,2:T(2,128)(2,1)}, u32[]{:S(2)}, u32[]{:S(2)}) collective-permute-start(bf16[1,2,16,4096]{3,1,0,2:T(2,128)(2,1)} %get-tuple-element.194), channel_id=1, source_target_pairs={{0,3},{1,2},{2,1},{3,0},{4,7},{5,6},{6,5},{7,4},{8,11},{9,10},{10,... | collective-permute-start | bytes 786440 | tf_op jit(solution)/shard_map/ppermute | solution.py:22
  385.2 120.9 %collective-permute-start.3 = (bf16[1,2,16,4096]{3,1,0,2:T(2,128)(2,1)}, bf16[1,2,16,4096]{3,1,0,2:T(2,128)(2,1)}, u32[]{:S(2)}, u32[]{:S(2)}) collective-permute-start(bf16[1,2,16,4096]{3,1,0,2:T(2,128)(2,1)} %get-tuple-element.193), channel_id=1, source_target_pairs={{0,4},{1,5},{2,6},{3,7},{4,0},{5,1},{6,2},{7,3},{8,12},{9,13},{10,... | collective-permute-start | bytes 786440 | tf_op jit(solution)/shard_map/ppermute | solution.py:22
  387.6 119.7 %collective-permute-start.4 = (bf16[1,2,16,4096]{3,1,0,2:T(2,128)(2,1)}, bf16[1,2,16,4096]{3,1,0,2:T(2,128)(2,1)}, u32[]{:S(2)}, u32[]{:S(2)}) collective-permute-start(bf16[1,2,16,4096]{3,1,0,2:T(2,128)(2,1)} %get-tuple-element.192), channel_id=1, source_target_pairs={{0,5},{1,4},{2,7},{3,6},{4,1},{5,0},{6,3},{7,2},{8,13},{9,12},{10,... | collective-permute-start | bytes 786440 | tf_op jit(solution)/shard_map/ppermute | solution.py:22
  389.7 2.9 copy-start.5
  492.9 57.8 %all-to-all-start.5 = ((bf16[8,40,2048]{2,1,0:T(8,128)(2,1)}), bf16[8,40,2048]{2,1,0:T(8,128)(2,1)S(1)}, u32[]{:S(2)}, u32[]{:S(2)}) async-start(bf16[8,40,2048]{2,1,0:T(8,128)(2,1)} %bitcast.32), calls=%async_computation.5 | async-start | bytes 2621440 | tf_op jit(solution)/shard_map/all_to_all | solution.py:177
  498.3 1.4 copy-start.11
  498.3 4.0 copy-start.10
  499.7 46.8 %collective-permute-start.5 = (bf16[1,2,16,4096]{3,1,0,2:T(2,128)(2,1)S(1)}, bf16[1,2,16,4096]{3,1,0,2:T(2,128)(2,1)S(1)}, u32[]{:S(2)}, u32[]{:S(2)}) collective-permute-start(bf16[1,2,16,4096]{3,1,0,2:T(2,128)(2,1)S(1)} %copy-done.11), channel_id=1, source_target_pairs={{0,6},{1,7},{2,4},{3,5},{4,2},{5,3},{6,0},{7,1},{8,14},{9,15},{10,... | collective-permute-start | bytes 786440 | tf_op jit(solution)/shard_map/ppermute | solution.py:22
  501.2 51.3 %copy-start.1 = (bf16[2048,8]{0,1:T(8,128)(2,1)S(1)}, bf16[2048,8]{0,1:T(8,128)(2,1)}, u32[]{:S(2)}) copy-start(bf16[2048,8]{0,1:T(8,128)(2,1)} %param.15) | copy-start | bytes 98308
  502.4 48.2 %collective-permute-start.6 = (bf16[1,2,16,4096]{3,1,0,2:T(2,128)(2,1)S(1)}, bf16[1,2,16,4096]{3,1,0,2:T(2,128)(2,1)S(1)}, u32[]{:S(2)}, u32[]{:S(2)}) collective-permute-start(bf16[1,2,16,4096]{3,1,0,2:T(2,128)(2,1)S(1)} %copy-done.10), channel_id=1, source_target_pairs={{0,7},{1,6},{2,5},{3,4},{4,3},{5,2},{6,1},{7,0},{8,15},{9,14},{10,... | collective-permute-start | bytes 786440 | tf_op jit(solution)/shard_map/ppermute | solution.py:22
  550.7 1.9 copy-start.7
Sparse Core Ops, SparseCore 0:
  65.7 57.6 all-gather.4
  126.2 88.3 all-gather.6
  216.2 107.2 all-gather.8
  325.4 58.2 all-gather.10
